TPU v7x, 32 devices: a whole 2x2x4 slice. The times are simulated.
32 devices in a mesh: dp: 8 (over y, x, core), seq: 4 (over z).
Axes of the slice: x: 2, y: 2, z: 4, core: 2. Of those that a mesh axis runs over, the one named last changes fastest.
Arguments:
- patches: bfloat16 [24, 532, 768], P('dp', 'seq'), may hold values from -6 to 6
- segments: int32 [24, 532], P('dp', 'seq'), may hold values from 0 to 3, as said below
- first_gain: bfloat16 [768], replicated, may hold values from 0.099609375 to 1.8984375
- first_bias: bfloat16 [768], replicated, may hold values from -1.75 to 1.75
- input_weight: bfloat16 [768, 2304], replicated, may hold values from -0.3125 to 0.3125
- query_bias: bfloat16 [768], replicated, may hold values from -3 to 3
- value_bias: bfloat16 [768], replicated, may hold values from -3 to 3
- output_weight: bfloat16 [768, 768], replicated, may hold values from -0.875 to 0.875
- output_bias: bfloat16 [768], replicated, may hold values from -1.75 to 1.75
- second_gain: bfloat16 [768], replicated, may hold values from 0.099609375 to 1.8984375
- second_bias: bfloat16 [768], replicated, may hold values from -1.75 to 1.75
- up_weight: bfloat16 [768, 3072], replicated, may hold values from -0.21875 to 0.21875
- up_bias: bfloat16 [3072], replicated, may hold values from -1.75 to 1.75
- down_weight: bfloat16 [3072, 768], replicated, may hold values from -0.109375 to 0.109375
- down_bias: bfloat16 [768], replicated, may hold values from -1.75 to 1.75
- cotangent: bfloat16 [24, 532, 768], P('dp', 'seq'), may hold values from -6 to 6
Outputs:
- block_output: bfloat16 [24, 532, 768], P('dp', 'seq')
- input_grad: float32 [24, 532, 768], P('dp', 'seq')
- first_gain_grad: float32 [768], replicated
- first_bias_grad: float32 [768], replicated
- input_weight_grad: float32 [768, 2304], P('dp', 'seq')
- query_bias_grad: float32 [768], replicated
- value_bias_grad: float32 [768], replicated
- output_weight_grad: float32 [768, 768], P('dp', 'seq')
- output_bias_grad: float32 [768], replicated
- second_gain_grad: float32 [768], replicated
- second_bias_grad: float32 [768], replicated
- up_weight_grad: float32 [768, 3072], P('dp', 'seq')
- up_bias_grad: float32 [3072], replicated
- down_weight_grad: float32 [3072, 768], P('dp', 'seq')
- down_bias_grad: float32 [768], replicated
Inputs may be any that keep to these rules, and one draw needn't show every extreme that they name: `segments`: 0 marks the padding at a strip's end and attends only to padding; other ids never fall along a strip and name packed documents; every strip holds padding and document 3; attention stays within equal ids.
All inputs are finite; a program needn't handle non-finite values.
Results may differ from a plain program's by a relative error of at most 0.012.
The roundings to bfloat16 on the way count: a program that leaves them out, or rounds other values in their place, can miss the bound.
Values may be sent and summed in bfloat16 or wider, within the bound.
A program may use at most 128 MiB of HBM per device.

v0:
```python
from functools import partial

import jax
import jax.numpy as jnp
from jax import lax
from jax.sharding import PartitionSpec as P

HEADS = 12
HEAD_DIM = 64


EPSILON = 1e-06
NEGATIVE = -1e30


def layer_norm(values, scales, offset):
    middle = jnp.mean(values, axis=-1, keepdims=True)
    centered = values - middle
    spread = jnp.mean(centered * centered, axis=-1, keepdims=True)
    return centered * lax.rsqrt(spread + EPSILON) * scales + offset


def column_sum(left, right):
    return lax.dot_general(
        left, right, (((0,), (0,)), ((), ())), preferred_element_type=jnp.float32
    )


def back_product(grads, weight):
    return lax.dot_general(
        grads, weight, (((1,), (1,)), ((), ())), preferred_element_type=jnp.float32
    )


def masked_scores(queries, keys, segment_row):
    raw = jnp.einsum(
        "qhd,khd->hqk", queries, keys, preferred_element_type=jnp.float32
    ) * HEAD_DIM ** (-0.5)
    same = segment_row[:, None] == segment_row[None, :]
    return jnp.where(same[None], raw, NEGATIVE)


def strip_forward(operands):
    queries, keys, values, segment_row = operands
    scores = masked_scores(queries, keys, segment_row)
    highest = jnp.max(scores, axis=-1, keepdims=True)
    exponent = jnp.exp(scores - highest)
    totals = jnp.sum(exponent, axis=-1, keepdims=True)
    probs = (exponent / totals).astype(jnp.bfloat16)
    attended = jnp.einsum("hqk,khd->qhd", probs, values, preferred_element_type=jnp.float32).astype(
        jnp.bfloat16
    )
    return (attended, highest + jnp.log(totals))


def strip_backward(operands):
    queries, keys, values, segment_row, log_totals, grad_att = operands
    scores = masked_scores(queries, keys, segment_row)
    probs = jnp.exp(scores - log_totals)
    grad_values = jnp.einsum(
        "hqk,qhd->khd", probs.astype(jnp.bfloat16), grad_att, preferred_element_type=jnp.float32
    )
    grad_probs = jnp.einsum("qhd,khd->hqk", grad_att, values, preferred_element_type=jnp.float32)
    inner = jnp.sum(probs * grad_probs, axis=-1, keepdims=True)
    grad_scores = (probs * (grad_probs - inner)).astype(jnp.bfloat16)
    factor = HEAD_DIM ** (-0.5)
    grad_queries = (
        jnp.einsum("hqk,khd->qhd", grad_scores, keys, preferred_element_type=jnp.float32) * factor
    )
    grad_keys = (
        jnp.einsum("hqk,qhd->khd", grad_scores, queries, preferred_element_type=jnp.float32)
        * factor
    )
    return jnp.stack([grad_queries, grad_keys, grad_values], axis=1).astype(jnp.bfloat16)


def on_device(
    patches,
    segments,
    first_gain,
    first_bias,
    input_weight,
    query_bias,
    value_bias,
    output_weight,
    output_bias,
    second_gain,
    second_bias,
    up_weight,
    up_bias,
    down_weight,
    down_bias,
    cotangent,
):
    strips, local_len, width = patches.shape
    rows = strips * local_len
    inputs = patches.astype(jnp.float32).reshape(rows, width)
    whole_ids = lax.all_gather(segments, "seq", axis=1, tiled=True)
    normed_first, in_pull = jax.vjp(
        layer_norm, inputs, first_gain.astype(jnp.float32), first_bias.astype(jnp.float32)
    )
    normed_in = normed_first.astype(jnp.bfloat16)
    bias_row = jnp.concatenate([query_bias, jnp.zeros_like(query_bias), value_bias]).astype(
        jnp.float32
    )
    mixed = (
        jnp.dot(normed_in, input_weight, preferred_element_type=jnp.float32) + bias_row
    ).astype(jnp.bfloat16)
    mixed = mixed.reshape(strips, local_len, 3, HEADS, HEAD_DIM)
    by_heads = lax.all_to_all(mixed, "seq", split_axis=3, concat_axis=1, tiled=True)
    queries = by_heads[:, :, 0]
    keys = by_heads[:, :, 1]
    values = by_heads[:, :, 2]
    attended, log_totals = lax.map(strip_forward, (queries, keys, values, whole_ids))
    attended = lax.all_to_all(attended, "seq", split_axis=1, concat_axis=2, tiled=True).reshape(
        rows, width
    )
    residual = (
        inputs
        + jnp.dot(attended, output_weight, preferred_element_type=jnp.float32)
        + output_bias.astype(jnp.float32)
    )
    normed_second, mid_pull = jax.vjp(
        layer_norm, residual, second_gain.astype(jnp.float32), second_bias.astype(jnp.float32)
    )
    normed_mid = normed_second.astype(jnp.bfloat16)
    upper = jnp.dot(normed_mid, up_weight, preferred_element_type=jnp.float32) + up_bias.astype(
        jnp.float32
    )
    activated, gelu_pull = jax.vjp(partial(jax.nn.gelu, approximate=False), upper)
    hidden = activated.astype(jnp.bfloat16)
    result = (
        residual
        + jnp.dot(hidden, down_weight, preferred_element_type=jnp.float32)
        + down_bias.astype(jnp.float32)
    )
    block_output = result.astype(jnp.bfloat16).reshape(strips, local_len, width)
    grad_low = cotangent.reshape(rows, width)
    grad_out = grad_low.astype(jnp.float32)
    down_weight_grad = column_sum(hidden, grad_low)
    down_bias_grad = jnp.sum(grad_out, axis=0)
    grad_upper = gelu_pull(back_product(grad_low, down_weight))[0].astype(jnp.bfloat16)
    up_weight_grad = column_sum(normed_mid, grad_upper)
    up_bias_grad = jnp.sum(grad_upper, axis=0, dtype=jnp.float32)
    grad_res_norm, second_gain_grad, second_bias_grad = mid_pull(
        back_product(grad_upper, up_weight)
    )
    grad_res = grad_out + grad_res_norm
    grad_proj = grad_res.astype(jnp.bfloat16)
    output_weight_grad = column_sum(attended, grad_proj)
    output_bias_grad = jnp.sum(grad_proj, axis=0, dtype=jnp.float32)
    grad_att = (
        back_product(grad_proj, output_weight)
        .astype(jnp.bfloat16)
        .reshape(strips, local_len, HEADS, HEAD_DIM)
    )
    grad_att = lax.all_to_all(grad_att, "seq", split_axis=2, concat_axis=1, tiled=True)
    grad_mixed = lax.map(strip_backward, (queries, keys, values, whole_ids, log_totals, grad_att))
    grad_mixed = lax.all_to_all(grad_mixed, "seq", split_axis=1, concat_axis=3, tiled=True).reshape(
        rows, 3 * width
    )
    input_weight_grad = column_sum(normed_in, grad_mixed)
    mixed_sums = jnp.sum(grad_mixed, axis=0, dtype=jnp.float32)
    query_bias_grad = mixed_sums[:width]
    value_bias_grad = mixed_sums[2 * width :]
    grad_in_norm, first_gain_grad, first_bias_grad = in_pull(back_product(grad_mixed, input_weight))
    input_grad = (grad_res + grad_in_norm).reshape(strips, local_len, width)
    vectors = lax.psum(
        (
            first_gain_grad,
            first_bias_grad,
            query_bias_grad,
            value_bias_grad,
            output_bias_grad,
            second_gain_grad,
            second_bias_grad,
            up_bias_grad,
            down_bias_grad,
        ),
        ("dp", "seq"),
    )
    pooled = (
        lax.psum_scatter(input_weight_grad, "dp", scatter_dimension=0, tiled=True),
        lax.psum_scatter(output_weight_grad, "dp", scatter_dimension=0, tiled=True),
        lax.psum_scatter(up_weight_grad, "dp", scatter_dimension=0, tiled=True),
        lax.psum_scatter(down_weight_grad, "dp", scatter_dimension=0, tiled=True),
    )
    summed = (
        lax.psum_scatter(pooled[0], "seq", scatter_dimension=1, tiled=True),
        lax.psum_scatter(pooled[1], "seq", scatter_dimension=1, tiled=True),
        lax.psum_scatter(pooled[2], "seq", scatter_dimension=1, tiled=True),
        lax.psum_scatter(pooled[3], "seq", scatter_dimension=1, tiled=True),
    )
    return (
        block_output,
        input_grad,
        vectors[0],
        vectors[1],
        summed[0],
        vectors[2],
        vectors[3],
        summed[1],
        vectors[4],
        vectors[5],
        vectors[6],
        summed[2],
        vectors[7],
        summed[3],
        vectors[8],
    )


def solution(mesh):
    return jax.shard_map(
        on_device,
        mesh=mesh,
        in_specs=(
            P("dp", "seq", None),
            P("dp", "seq"),
            P(),
            P(),
            P(),
            P(),
            P(),
            P(),
            P(),
            P(),
            P(),
            P(),
            P(),
            P(),
            P(),
            P("dp", "seq", None),
        ),
        out_specs=(
            P("dp", "seq", None),
            P("dp", "seq", None),
            P(),
            P(),
            P("dp", "seq"),
            P(),
            P(),
            P("dp", "seq"),
            P(),
            P(),
            P(),
            P("dp", "seq"),
            P(),
            P("dp", "seq"),
            P(),
        ),
        check_vma=False,
    )
```

profile of v0, /device:TPU:0, one launch (start us, length us, event | category | flops | bytes accessed | tf_op | source)
XLA Modules:
  0.0 755.3 jit_solution(16342300128980591202)
XLA Ops:
  20.8 6.7 reshape.318
  27.4 8.7 %copy.80 = bf16[3,133,3,12,64]{1,4,2,0,3:T(8,128)(2,1)} copy(bf16[3,133,3,12,64]{4,3,2,1,0:T(8,128)(2,1)} %reshape.318) | data formatting | bytes 3677184 | tf_op jit(solution)/shard_map/reshape | solution.py:109
  36.2 6.4 all-to-all-start
  42.6 84.5 %all-gather = s32[4,133,3]{1,2,0:T(4,128)S(1)} all-gather(s32[1,133,3]{1,2,0:T(4,128)S(1)} %bitcast.171), channel_id=1, replica_groups=mesh['dp'=8,'seq'=4] {'seq'}, dimensions={0}, use_global_device_ids=true | all-gather | bytes 7980 | tf_op jit(solution)/shard_map/all_gather | solution.py:98
  128.5 7.1 copy.82
  135.6 6.8 all_to_all.51
  145.6 21.0 %while.22 = (s32[]{:T(128)}, bf16[3,532,3,64]{1,3,2,0:T(8,128)(2,1)}, f32[3,3,532,1]{2,1,3,0:T(4,128)}, bf16[3,532,3,64]{1,3,2,0:T(8,128)(2,1)}, s32[3,532]{1,0:...) while((s32[]{:T(128)}, bf16[3,532,3,64]{1,3,2,0:T(8,128)(2,1)}, ...), condition=%wide.region_5.6_spmd, body=%wide.region_2.5_spmd.sunk | while | flops 227934864 | bytes 12367461 | solution.py:114
  174.1 4.7 all-to-all-start.1
  185.4 7.4 all-to-all-done.1
  207.3 4.7 fusion.72
  212.0 15.6 %convert_reduce_fusion.1 = (f32[3072]{0:T(1024)}, bf16[399,3072]{1,0:T(8,128)(2,1)S(1)}, f32[399,3072]{1,0:T(8,128)}) fusion(f32[399,3072]{1,0:T(8,128)S(1)} %fusion.72, f32[3072]{0:T(1024)S(1)} %copy-done.15, bf16[399,768]{1,0:T(8,128)(2,1)S(1)} %copy-done.5, bf16[3072,768]{1,0:T(8,128)(2,1)S(1)} %bitcast.175), kind=kOutput, calls=%fused_computation.67 | convolution fusion | flops 1974644736 | bytes 17613312 | tf_op jit(solution)/shard_map/dot_general | solution.py:30
  250.3 21.5 %all-to-all-done.2 = bf16[3,133,12,64]{1,3,0,2:T(8,128)(2,1)} async-done(((bf16[3,133,12,64]{1,3,0,2:T(8,128)(2,1)}), bf16[3,133,12,64]{1,3,0,2:T(8,128)(2,1)}, u32[]{:S(2)}, u32[]{:S(2)}) %all-to-all-start.2) | async-done | bytes 612896 | tf_op jit(solution)/shard_map/all_to_all | solution.py:157
  278.2 36.7 %while.23 = (s32[]{:T(128)}, bf16[3,532,3,3,64]{1,4,3,2,0:T(8,128)(2,1)}, bf16[3,532,3,64]{1,3,2,0:T(8,128)(2,1)}, s32[3,532]{1,0:T(4,128)S(1)}, bf16[3,532,3,64...) while((s32[]{:T(128)}, ...), condition=%wide.region_12.13_spmd, body=%wide.region_10.12_spmd.sunk | while | flops 558772864 | bytes 34360440 | solution.py:158
  314.9 8.0 %copy.89 = bf16[3,532,3,3,64]{4,3,2,0,1:T(4,128)(2,1)} copy(bf16[3,532,3,3,64]{1,4,3,2,0:T(8,128)(2,1)} %get-tuple-element.97) | data formatting | bytes 3677184 | tf_op jit(solution)/shard_map/while | solution.py:158
  322.9 7.7 %reshape.337 = bf16[4,2,114912]{2,1,0:T(2,128)(2,1)} reshape(bf16[532,3,3,3,64]{4,3,2,1,0:T(4,128)(2,1)} %bitcast.160) | data formatting | bytes 3677184
  330.6 4.4 all-to-all-start.3
  339.6 37.1 %all-to-all-done.3 = bf16[4,2,114912]{2,1,0:T(2,128)(2,1)} async-done(((bf16[4,2,114912]{2,1,0:T(2,128)(2,1)}), bf16[4,2,114912]{2,1,0:T(2,128)(2,1)}, u32[]{:S(2)}, u32[]{:S(2)}) %all-to-all-start.3) | async-done | bytes 1838624 | tf_op jit(solution)/shard_map/all_to_all | solution.py:159
  376.8 9.4 %reshape.338 = bf16[532,3,3,3,64]{4,3,2,1,0:T(4,128)(2,1)} reshape(bf16[4,2,114912]{2,1,0:T(2,128)(2,1)} %all-to-all-done.3) | data formatting | bytes 3677184
  386.2 6.2 copy.108
  392.5 8.9 %reshape.323 = bf16[399,2304]{1,0:T(8,128)(2,1)} reshape(bf16[3,133,3,4,3,64]{5,4,3,2,1,0:T(4,128)(2,1)} %bitcast.161) | data formatting | bytes 3677184 | tf_op jit(solution)/shard_map/reshape | solution.py:159
  401.3 6.6 fusion.79
  408.7 9.6 %fusion.71 = f32[768,3072]{1,0:T(8,128)} fusion(bf16[399,3072]{1,0:T(8,128)(2,1)} %copy-done.38, f32[399,768]{1,0:T(8,128)} %copy-done.4, f32[768]{0:T(1024)} %convert_element_type.107, f32[768]{0:T(1024)S(1)} %copy-done.29, f32[399]{0:T(512)S(1)} %copy-done.34, f32[399]{0:T(512)S(1)} %copy-done.22), kind=kOutput, calls=%fused_computation.128 | convolution fusion | flops 1884250368 | bytes 13123704 | tf_op jit(solution)/shard_map/dot_general | solution.py:24
  419.0 6.1 multiply_convert_fusion.1
  426.6 5.1 fusion.81
  434.1 38.8 %reduce-scatter.15.cloned.1.call-done = f32[96,2304]{1,0:T(8,128)} async-done(((f32[768,2304]{1,0:T(8,128)}), f32[96,2304]{1,0:T(8,128)}) %reduce-scatter.15.cloned.1.call-update) | async-done | bytes 884752 | tf_op jit(solution)/shard_map/reduce_scatter | solution.py:183
  475.6 77.4 %reduce-scatter.19.cloned.1.call-done = f32[96,3072]{1,0:T(8,128)} async-done(((f32[768,3072]{1,0:T(8,128)}), f32[96,3072]{1,0:T(8,128)}) %reduce-scatter.19.cloned.1.call-update) | async-done | bytes 1179664 | tf_op jit(solution)/shard_map/reduce_scatter | solution.py:185
  554.8 6.3 fusion.63
  563.4 69.3 %reduce-scatter.23.cloned.1.call-done = f32[384,768]{1,0:T(8,128)} async-done(((f32[3072,768]{1,0:T(8,128)}), f32[384,768]{1,0:T(8,128)}) %reduce-scatter.23.cloned.1.call-update) | async-done | bytes 1179664 | tf_op jit(solution)/shard_map/reduce_scatter | solution.py:186
  645.2 5.0 convert_reduce_fusion
  651.0 43.6 %all-reduce = (f32[768]{0:T(1024)}, f32[768]{0:T(1024)}, f32[768]{0:T(1024)}, f32[768]{0:T(1024)}, f32[768]{0:T(1024)}, /*index=5*/f32[768]{0:T(1024)}, f32[768]{0:T(1024)}, f32[3072]{0:T(1024)}, f32[768]{0:T(1024)}) all-reduce(f32[768]{0:T(1024)} %get-tuple-element.175, ...), channel_id=1, replica_groups=mesh['dp'=8,'seq'=4] {'dp','seq'}, use_global_device_ids=true, to_apply=%region_16.17 | all-reduce | flops 9216 | bytes 73728 | tf_op jit(solution)/shard_map/psum | solution.py:168
  698.1 19.2 %reduce-scatter.21.cloned.1.call-done = f32[96,768]{1,0:T(8,128)} async-done(((f32[96,3072]{1,0:T(8,128)}), f32[96,768]{1,0:T(8,128)}) %reduce-scatter.21.cloned.1.call-update) | async-done | bytes 294928 | tf_op jit(solution)/shard_map/reduce_scatter | solution.py:191
  717.3 30.9 %reduce-scatter.29.cloned.1.call-done = f32[192,384]{1,0:T(8,128)} async-done(((f32[768,384]{1,0:T(8,128)}), f32[192,384]{1,0:T(8,128)}) %reduce-scatter.29.cloned.1.call-update) | async-done | bytes 294928
  (224 shorter events, 166.1 us)
Async XLA Ops:
  7.2 9.3 %copy-start = (bf16[768,2304]{1,0:T(8,128)(2,1)S(1)}, bf16[768,2304]{1,0:T(8,128)(2,1)}, u32[]{:S(2)}) copy-start(bf16[768,2304]{1,0:T(8,128)(2,1)} %param.24) | copy-start | bytes 10616836
  10.9 9.9 %copy-start.13 = (f32[3,133]{1,0:T(4,128)}, f32[3,133]{1,0:T(4,128)S(1)}, u32[]{:S(2)}) copy-start(f32[3,133]{1,0:T(4,128)S(1)} %broadcast_multiply_fusion) | copy-start | bytes 4792
  13.7 7.1 copy-start.26
  14.3 6.4 copy-start.17
  36.2 6.5 copy-start.35
  36.2 92.4 %all-to-all-start = ((bf16[3,133,3,12,64]{1,4,2,0,3:T(8,128)(2,1)}), bf16[3,133,3,12,64]{1,4,2,0,3:T(8,128)(2,1)}, u32[]{:S(2)}, u32[]{:S(2)}) async-start(bf16[3,133,3,12,64]{1,4,2,0,3:T(8,128)(2,1)} %copy.80), calls=%async_computation | async-start | bytes 7077888 | tf_op jit(solution)/shard_map/all_to_all | solution.py:110
  174.1 18.7 %all-to-all-start.1 = ((bf16[4,2,38304]{2,1,0:T(2,128)(2,1)}), bf16[4,2,38304]{2,1,0:T(2,128)(2,1)}, u32[]{:S(2)}, u32[]{:S(2)}) async-start(bf16[4,2,38304]{2,1,0:T(2,128)(2,1)} %reshape.335), calls=%async_computation.1 | async-start | bytes 1228800 | tf_op jit(solution)/shard_map/all_to_all | solution.py:115
  204.1 7.8 %slice-start.2 = ((s8[4718592]{0:T(1024)(128)(4,1)}), s8[4194304]{0:T(1024)(128)(4,1)S(1)}, s32[]{:S(2)}) async-start(s8[4718592]{0:T(1024)(128)(4,1)} %bitcast.174), calls=%async_computation.22 | async-start | bytes 8388608
  206.9 23.7 %copy-start.4 = (f32[399,768]{1,0:T(8,128)}, f32[399,768]{1,0:T(8,128)S(1)}, u32[]{:S(2)}) copy-start(f32[399,768]{1,0:T(8,128)S(1)} %get-tuple-element.239) | copy-start | bytes 3677188
  206.9 23.7 %copy-start.21 = (f32[399]{0:T(512)}, f32[399]{0:T(512)S(1)}, u32[]{:S(2)}) copy-start(f32[399]{0:T(512)S(1)} %broadcast_multiply_fusion.1) | copy-start | bytes 4792
  207.2 23.4 %copy-start.33 = (f32[399]{0:T(512)}, f32[399]{0:T(512)S(1)}, u32[]{:S(2)}) copy-start(f32[399]{0:T(512)S(1)} %fusion.69) | copy-start | bytes 4792
  207.3 20.4 %slice-start = ((s8[4718592]{0:T(1024)(128)(4,1)}), s8[4194304]{0:T(1024)(128)(4,1)S(1)}, s32[]{:S(2)}) async-start(s8[4718592]{0:T(1024)(128)(4,1)} %bitcast.172), calls=%async_computation.20 | async-start | bytes 8388608
  212.0 15.6 %copy-start.9 = (f32[399,3072]{1,0:T(8,128)}, f32[399,3072]{1,0:T(8,128)S(1)}, u32[]{:S(2)}) copy-start(f32[399,3072]{1,0:T(8,128)S(1)} %fusion.72) | copy-start | bytes 14708740
  212.0 15.6 %slice-start.1 = ((s8[4718592]{0:T(1024)(128)(4,1)}), s8[524288]{0:T(1024)(128)(4,1)S(1)}, s32[]{:S(2)}) async-start(s8[4718592]{0:T(1024)(128)(4,1)} %bitcast.172), calls=%async_computation.21 | async-start | bytes 1048576
  242.2 29.6 %all-to-all-start.2 = ((bf16[3,133,12,64]{1,3,0,2:T(8,128)(2,1)}), bf16[3,133,12,64]{1,3,0,2:T(8,128)(2,1)}, u32[]{:S(2)}, u32[]{:S(2)}) async-start(bf16[3,133,12,64]{1,3,0,2:T(8,128)(2,1)} %copy.86), calls=%async_computation.2 | async-start | bytes 2359296 | tf_op jit(solution)/shard_map/all_to_all | solution.py:157
  246.5 185.5 %reduce-scatter.17.cloned.1.call-start = ((), (), s32[]{:S(2)}) async-start(), calls=%async_computation.13 | async-start | bytes 2654208 | tf_op jit(solution)/shard_map/reduce_scatter | solution.py:184
  322.9 12.4 %copy-start.14 = (f32[3,133]{1,0:T(4,128)S(1)}, f32[3,133]{1,0:T(4,128)}, u32[]{:S(2)}) copy-start(f32[3,133]{1,0:T(4,128)} %copy-done.13) | copy-start | bytes 4792
  322.9 12.4 %copy-start.18 = (f32[768]{0:T(1024)S(1)}, f32[768]{0:T(1024)}, u32[]{:S(2)}) copy-start(f32[768]{0:T(1024)} %copy-done.17) | copy-start | bytes 9220
  322.9 12.4 %copy-start.25 = (f32[3,133]{1,0:T(4,128)S(1)}, f32[3,133]{1,0:T(4,128)}, u32[]{:S(2)}) copy-start(f32[3,133]{1,0:T(4,128)} %get-tuple-element.236) | copy-start | bytes 4792
  322.9 12.4 %copy-start.27 = (f32[768]{0:T(1024)S(1)}, f32[768]{0:T(1024)}, u32[]{:S(2)}) copy-start(f32[768]{0:T(1024)} %copy-done.26) | copy-start | bytes 9220
  330.6 46.1 %all-to-all-start.3 = ((bf16[4,2,114912]{2,1,0:T(2,128)(2,1)}), bf16[4,2,114912]{2,1,0:T(2,128)(2,1)}, u32[]{:S(2)}, u32[]{:S(2)}) async-start(bf16[4,2,114912]{2,1,0:T(2,128)(2,1)} %reshape.337), calls=%async_computation.3 | async-start | bytes 3678208 | tf_op jit(solution)/shard_map/all_to_all | solution.py:159
  335.0 137.9 %reduce-scatter.15.cloned.1.call-start = ((), (), s32[]{:S(2)}) async-start(), calls=%async_computation.12 | async-start | bytes 7962624 | tf_op jit(solution)/shard_map/reduce_scatter | solution.py:183
  408.0 144.9 %reduce-scatter.19.cloned.1.call-start = ((), (), s32[]{:S(2)}) async-start(), calls=%async_computation.14 | async-start | bytes 10616832 | tf_op jit(solution)/shard_map/reduce_scatter | solution.py:185
  418.3 214.5 %reduce-scatter.23.cloned.1.call-start = ((), (), s32[]{:S(2)}) async-start(), calls=%async_computation.16 | async-start | bytes 10616832 | tf_op jit(solution)/shard_map/reduce_scatter | solution.py:186
  419.0 7.5 copy-start.6
  431.7 121.3 %copy-start.37 = (bf16[768]{0:T(1024)(128)(2,1)S(1)}, bf16[768]{0:T(1024)(128)(2,1)}, u32[]{:S(2)}) copy-start(bf16[768]{0:T(1024)(128)(2,1)} %param.34) | copy-start | bytes 4612
  431.7 262.9 %reduce-scatter.27.cloned.1.call-start = ((), (), s32[]{:S(2)}) async-start(), calls=%async_computation.18 | async-start | bytes 491520
  434.0 262.3 %reduce-scatter.25.cloned.1.call-start = ((), (), s32[]{:S(2)}) async-start(), calls=%async_computation.17 | async-start | bytes 1474560
  475.5 241.8 %reduce-scatter.21.cloned.1.call-start = ((), (), s32[]{:S(2)}) async-start(), calls=%async_computation.15 | async-start | bytes 1474560 | tf_op jit(solution)/shard_map/reduce_scatter | solution.py:191
  553.0 195.3 %reduce-scatter.29.cloned.1.call-start = ((), (), s32[]{:S(2)}) async-start(), calls=%async_computation.19 | async-start | bytes 1474560
  561.1 74.4 %copy-start.30 = (f32[399]{0:T(512)S(1)}, f32[399]{0:T(512)}, u32[]{:S(2)}) copy-start(f32[399]{0:T(512)} %div.47) | copy-start | bytes 4792
  561.1 74.4 %copy-start.32 = (f32[399]{0:T(512)S(1)}, f32[399]{0:T(512)}, u32[]{:S(2)}) copy-start(f32[399]{0:T(512)} %copy-done.31) | copy-start | bytes 4792
  (25 other events, 62.4 us)
Sparse Core Ops, SparseCore 0:
  250.7 44.0 reduce-scatter.16
  408.1 64.7 reduce-scatter.14
  476.4 76.4 reduce-scatter.18
  556.3 76.4 reduce-scatter.22
  634.9 20.5 reduce-scatter.26
  657.8 28.4 reduce-scatter.24
  689.3 27.9 reduce-scatter.20
  720.3 27.8 reduce-scatter.28
where the time goes:
time: 762 us; the launch traced here: 755 us
  waiting for transfers between devices  302 us (40%)
  local copies, waits for them, and re-layouts  138 us (18%)
  blocking collectives  128 us (17%)
  matrix products  110 us (14%)
  other arithmetic  41.3 us (5%)
  starting transfers between devices  20.8 us (3%)
  between operations  14.9 us (2%)
    all_gather x1, blocking collectives, on_device(): whole_ids = lax.all_gather(segments, 'seq', axis=1, tiled=True)  84.5 us
    reduce_scatter x1, waiting for transfers between devices, on_device(): lax.psum_scatter(up_weight_grad, 'dp', scatter_dimension=0, tiled=True)  77.4 us
    reduce_scatter x1, waiting for transfers between devices, on_device(): lax.psum_scatter(down_weight_grad, 'dp', scatter_dimension=0, tiled=True)  69.3 us
    psum x1, blocking collectives, on_device(): lax.psum((first_gain_grad, first_bias_grad, query_bias_grad, value_bias_g...  43.6 us
    unnamed x94, local copies, waits for them, and re-layouts  42.6 us
    reduce_scatter x1, waiting for transfers between devices, on_device(): lax.psum_scatter(input_weight_grad, 'dp', scatter_dimension=0, tiled=True)  38.8 us
    all_to_all x1, waiting for transfers between devices, on_device(): lax.all_to_all(grad_mixed, 'seq', split_axis=1, concat_axis=3, tiled=True)  37.1 us
    unnamed x11, waiting for transfers between devices  31 us
  transfers between devices with their start and end apart: 12, of which 8 were waited for; matrix products, arithmetic and copies ran while one was open for 21% of the time, Pallas kernels for 0%

commit v1 on v0

v1 whole, which is shorter than its diff:
```python
import functools

import jax
import jax.numpy as jnp
from jax import lax
from jax.experimental import pallas as pl
from jax.experimental.pallas import tpu as pltpu
from jax.sharding import PartitionSpec as P

F32 = jnp.float32
BF = jnp.bfloat16
EPS = 1e-6
VL = 60 << 20
PART = 136

def nn(a,b): return lax.dot_general(a,b,(((1,),(0,)),((),())),preferred_element_type=F32)
def nt(a,b): return lax.dot_general(a,b,(((1,),(1,)),((),())),preferred_element_type=F32)
def tn(a,b): return lax.dot_general(a,b,(((0,),(0,)),((),())),preferred_element_type=F32)

def norm_parts(v):
    mid=jnp.mean(v,axis=-1,keepdims=True)
    c=v-mid
    r=lax.rsqrt(jnp.mean(c*c,axis=-1,keepdims=True)+EPS)
    return c*r,r

G1, B1, QB, VB, OB, G2, B2, DB = range(8)


def ka_kernel(x_ref, eq_ref, ek_ref, par_ref, wq_ref, wk_ref, wv_ref, qb_ref, vb_ref, wo_ref,
              q_out, k_out, v_out, att_out, lse_out, nmid_out, res_out, acc, nin_ref):
    i = pl.program_id(0)
    rows = x_ref.shape[0]

    @pl.when(i == 0)
    def _():
        xh, _r = norm_parts(x_ref[...].astype(F32))
        nin_ref[...] = (xh * par_ref[G1:G1 + 1] + par_ref[B1:B1 + 1]).astype(BF)
        acc[...] = jnp.zeros_like(acc)

    nin = nin_ref[...]
    q_out[...] = (nn(nin, wq_ref[...]) + qb_ref[QB:QB + 1]).astype(BF)
    k_out[...] = nn(nin, wk_ref[...]).astype(BF)
    v_out[...] = (nn(nin, wv_ref[...]) + vb_ref[VB:VB + 1]).astype(BF)
    lane = lax.broadcasted_iota(jnp.int32, (rows, 128), 1)
    eq = eq_ref[...]
    ek = ek_ref[...]
    for pair in range(2):
        cols = slice(128 * pair, 128 * pair + 128)
        qp = q_out[:, cols] * jnp.asarray(0.125, BF)
        kp = jnp.concatenate([k_out[:, cols], ek], axis=1)
        vp = v_out[:, cols]
        zero = jnp.zeros_like(qp)
        both = jnp.concatenate([jnp.concatenate([jnp.where(lane < 64, qp, zero), eq], axis=1),
                                jnp.concatenate([jnp.where(lane < 64, zero, qp), eq], axis=1)], axis=0)
        s = nt(both, kp)
        m = jnp.max(s, axis=-1, keepdims=True)
        e = jnp.exp(s - m)
        t = jnp.sum(e, axis=-1, keepdims=True)
        p = (e * (1.0 / t)).astype(BF)
        o = nn(p, vp)
        log = m + jnp.log(t)
        lse_out[:, 2 * pair:2 * pair + 1] = log[:rows]
        lse_out[:, 2 * pair + 1:2 * pair + 2] = log[rows:]
        att_out[:, cols] = jnp.where(lane < 64, o[:rows], o[rows:]).astype(BF)
    acc[...] += nn(att_out[...], wo_ref[...])

    @pl.when(i == pl.num_programs(0) - 1)
    def _():
        res = x_ref[...].astype(F32) + acc[...] + par_ref[OB:OB + 1]
        res_out[...] = res
        xh, _r = norm_parts(res)
        nmid_out[...] = (xh * par_ref[G2:G2 + 1] + par_ref[B2:B2 + 1]).astype(BF)


def ka(x, eq, ek, par, wi, wo):
    rows, D = x.shape
    full = lambda a: pl.BlockSpec(a.shape, lambda i: (0,) * a.ndim)
    n = 3
    blk = pl.BlockSpec((rows, 256), lambda i: (0, i))
    whole = pl.BlockSpec((rows, D), lambda i: (0, 0))
    S = jax.ShapeDtypeStruct
    wcol = lambda j: pl.BlockSpec((D, 256), lambda i: (0, n * j + i))
    pcol = pl.BlockSpec((8, 256), lambda i: (0, i))
    return pl.pallas_call(
        ka_kernel, grid=(n,),
        in_specs=[full(x), full(eq), full(ek), full(par), wcol(0), wcol(1), wcol(2), pcol, pcol,
                  pl.BlockSpec((256, D), lambda i: (i, 0))],
        out_specs=[blk, blk, blk, blk, pl.BlockSpec((rows, 128), lambda i: (0, i)), whole, whole],
        out_shape=[S((rows, D), BF)] * 4 + [S((rows, 384), F32), S((rows, D), BF), S((rows, D), F32)],
        scratch_shapes=[pltpu.VMEM((rows, D), F32), pltpu.VMEM((rows, D), BF)],
        name="attend_forward",
        compiler_params=pltpu.CompilerParams(vmem_limit_bytes=VL),
        cost_estimate=pl.CostEstimate(flops=17_000_000 * 1000, bytes_accessed=12_000_000, transcendentals=0),
    )(x, eq, ek, par, wi, wi, wi, par, par, wo)


def gelu_parts(u):
    a=jnp.abs(u)
    t=1.0/(a*(0.3275911*0.7071067811865476)+1.0)
    e=jnp.exp(u*u*-0.5)
    w=((((0.5*1.061405429*t-0.5*1.453152027)*t+0.5*1.421413741)*t-0.5*0.284496736)*t+0.5*0.254829592)*t*e
    phi=jnp.where(u>=0,1.0-w,w)
    return u*phi,phi+u*e*0.3989422804014327

def kb_kernel(sb,first,last,rel_ref,nmid_ref,cot_ref,*refs):
    nt_=2*sb
    wu_refs=refs[:nt_]; ub_refs=refs[nt_:2*nt_]; wd_refs=refs[2*nt_:3*nt_]
    down_in,dn_in,down_ref,dn_ref,keep_ref,send_ref,ubg_ref,nmt,cott,tmp=refs[3*nt_:3*nt_+10]
    down_acc=refs[-1] if last else down_ref
    i=pl.program_id(0)
    dp=rel_ref[0]; z=rel_ref[1]
    @pl.when(i==0)
    def _():
        nmt[...]=nmid_ref[...].T
        cott[...]=cot_ref[...].T
        down_acc[...]=down_in[...]
        if first:
            down_acc[...]+=dn_in[DB:DB+1]
            dn_ref[...]=jnp.zeros_like(dn_ref)
        else:
            dn_ref[...]=dn_in[...]
    nm=nmid_ref[...]; cot=cot_ref[...]
    wu=jnp.concatenate([r[...] for r in wu_refs],axis=1)
    wd=jnp.concatenate([r[...] for r in wd_refs],axis=0)
    ub=jnp.concatenate([r[...] for r in ub_refs],axis=1)
    u=nn(nm,wu)+ub
    act,der=gelu_parts(u)
    hid=act.astype(BF)
    gu=(nt(cot,wd)*der).astype(BF)
    down_acc[...]+=nn(hid,wd)
    dn_ref[...]+=nt(gu,wu)
    rows=nm.shape[0]
    ubg_ref[...]=jnp.sum(gu.astype(F32),axis=0,keepdims=True)
    tmp[...]=nn(nmt[...],gu).astype(BF)
    for r in range(8):
        out=(keep_ref,send_ref)[r&1]
        at=(r>>1&1)*2+(r>>2)
        rows_at=pl.ds(pl.multiple_of(lax.bitwise_xor(dp,r)*96,32),96)
        for k in range(sb):
            slot=lax.bitwise_xor(sb*i+k,z)
            for h in range(2):
                lanes=slice(256*k+128*h,256*k+128*h+128)
                out[0,at,slot,96*h:96*h+96,:]=tmp[rows_at,lanes]
    tmp[...]=nn(cott[...],hid).astype(BF)
    for k in range(sb):
        for p in range(2):
            out=(keep_ref,send_ref)[p]
            h=lax.bitwise_xor(dp&1,p)
            at=lax.bitwise_xor(2*(sb*i+k)+h,dp)>>1
            for s in range(4):
                out[1,at,lax.bitwise_xor(z,s)]=tmp[192*s:192*s+192,pl.ds(pl.multiple_of(256*k+128*h,128),128)]

    if last:
        @pl.when(i==pl.num_programs(0)-1)
        def _(): down_ref[...]=down_acc[...].astype(BF)

def kb(j,rel,nmid,cot,wu,ub,wd,down,dn,sb=4):
    first,last=j==0,j==2
    rows,D=nmid.shape
    cst=lambda shape: pl.BlockSpec(shape,lambda i,*_:(0,)*len(shape))
    S=jax.ShapeDtypeStruct
    offs=[6*k+3*h+j for k in range(sb) for h in range(2)]
    col=lambda o,n: pl.BlockSpec((n,128),lambda i,*_:(0,6*sb*i+o))
    row=lambda o: pl.BlockSpec((128,D),lambda i,*_:(6*sb*i+o,0))
    n=len(offs)
    return pl.pallas_call(functools.partial(kb_kernel,sb,first,last),
      grid_spec=pltpu.PrefetchScalarGridSpec(num_scalar_prefetch=1,grid=(4//sb,),
      in_specs=[cst((rows,D)),cst((rows,D))]+[col(o,D) for o in offs]+[col(o,1) for o in offs]+[row(o) for o in offs]+[cst((rows,D)),cst(dn.shape)],
      out_specs=[cst((rows,D)),cst((rows,D)),cst((2,4,4,192,128)),cst((2,4,4,192,128)),pl.BlockSpec((1,256*sb),lambda i,*_:(0,i))],
      scratch_shapes=[pltpu.VMEM((D,rows),BF)]*2+[pltpu.VMEM((D,256*sb),BF)]+([pltpu.VMEM((rows,D),F32)] if last else [])),
      out_shape=[S((rows,D),BF if last else F32),S((rows,D),F32)]+[S((2,4,4,192,128),BF)]*2+[S((1,1024),F32)],
      name="feed_forward",
      cost_estimate=pl.CostEstimate(flops=14_000_000*1000,bytes_accessed=16_000_000,transcendentals=0),
      compiler_params=pltpu.CompilerParams(vmem_limit_bytes=VL),
    )(rel,nmid,cot,*([wu]*n),*([ub]*n),*([wd]*n),down,dn)

def norm_back(dy,g,xh,r):
    dx=dy*g
    return r*(dx-jnp.mean(dx,axis=-1,keepdims=True)-xh*jnp.mean(dx*xh,axis=-1,keepdims=True))

def col(v): return jnp.sum(v,axis=0,keepdims=True)

def kc_kernel(rel_ref,x_ref,cot_ref,res_ref,dn_ref,att_ref,q_ref,k_ref,v_ref,lse_ref,eq_ref,ek_ref,wo_ref,wq_ref,wk_ref,wv_ref,par_ref,
              ing_ref,keep_ref,send_ref,vec_ref, gres,gproj,nint,acc,tmp,dm):
    i=pl.program_id(0)
    dp=rel_ref[0]
    rows=x_ref.shape[0]
    def scatter(c,order,val):
        tmp[...]=val
        for r in range(8):
            xb,yb=r>>1&1,r>>2
            at=jnp.where(order==0,2*xb+yb,2*yb+xb)
            (keep_ref,send_ref)[r&1][c,at]=tmp[pl.ds(pl.multiple_of(lax.bitwise_xor(dp,r)*96,32),96),:]
    @pl.when(i==0)
    def _():
        cot=cot_ref[...].astype(F32)
        dy=dn_ref[...]
        xh,r=norm_parts(res_ref[...])
        g=cot+norm_back(dy,par_ref[G2:G2+1],xh,r)
        gres[...]=g
        gb=g.astype(BF)
        gproj[...]=gb
        vec_ref[4:5]=col(gb.astype(F32))
        vec_ref[5:6]=col(dy*xh)
        vec_ref[6:7]=col(dy)
        vec_ref[7:8]=col(cot)
        scatter(3,0,tn(att_ref[...],gb).astype(BF))
        xh,r=norm_parts(x_ref[...].astype(F32))
        nint[...]=(xh*par_ref[G1:G1+1]+par_ref[B1:B1+1]).astype(BF).T
        acc[...]=jnp.zeros_like(acc)
    da=nt(gproj[...],wo_ref[...]).astype(BF)
    lane=lax.broadcasted_iota(jnp.int32,(rows,128),1)
    ek=ek_ref[...]
    for pair in range(2):
        cols=slice(128*pair,128*pair+128)
        qp=q_ref[:,cols]*jnp.asarray(0.125,BF); kp=k_ref[:,cols]
        zero=jnp.zeros_like(qp)
        qm=jnp.concatenate([jnp.where(lane<64,qp,zero),jnp.where(lane<64,zero,qp)],axis=0)
        ext=[]
        for h in range(2):
            l=lse_ref[:,2*pair+h:2*pair+h+1]
            hi=l.astype(BF); l=l-hi.astype(F32)
            mid=l.astype(BF); lo=(l-mid.astype(F32)).astype(BF)
            ext.append(jnp.where(lane==5,-hi,jnp.where(lane==6,-mid,jnp.where(lane==7,-lo,eq_ref[...]))))
        st=nt(jnp.concatenate([kp,ek],axis=1),jnp.concatenate([qm,jnp.concatenate(ext,axis=0)],axis=1))
        p=jnp.exp(st)
        dap=da[:,cols]
        dob=jnp.concatenate([jnp.where(lane<64,dap,zero),jnp.where(lane<64,zero,dap)],axis=0)
        dpt=nt(v_ref[:,cols],dob)
        dv=nn(p.astype(BF),dob)
        inner=jnp.sum(p*dpt,axis=0,keepdims=True)
        ds=(p*(dpt-inner)).astype(BF)
        dk=nn(ds,qm)
        dq=tn(ds,kp)*0.125
        dm[:,128*pair:128*pair+128]=jnp.where(lane<64,dq[:rows],dq[rows:]).astype(BF)
        dm[:,256+128*pair:256+128*pair+128]=dk.astype(BF)
        dm[:,512+128*pair:512+128*pair+128]=dv.astype(BF)
    w=jnp.concatenate([wq_ref[...],wk_ref[...],wv_ref[...]],axis=1)
    acc[...]+=nt(dm[...],w)
    at=pl.ds(pl.multiple_of(256*i,256),256)
    vec_ref[2:3,at]=col(dm[:,0:256].astype(F32))
    vec_ref[3:4,at]=col(dm[:,512:768].astype(F32))
    scatter(i,jnp.minimum(i,1),nn(nint[...],dm[...]).astype(BF))
    @pl.when(i==pl.num_programs(0)-1)
    def _():
        xh,r=norm_parts(x_ref[...].astype(F32))
        dy=acc[...]
        vec_ref[0:1]=col(dy*xh)
        vec_ref[1:2]=col(dy)
        ing_ref[...]=(gres[...]+norm_back(dy,par_ref[G1:G1+1],xh,r)).astype(BF)

def kc(rel,x,cot,res,dn,att,q,k,v,lse,eq,ek,wo,wi,par):
    rows,D=x.shape
    cst=lambda shape: pl.BlockSpec(shape,lambda i,*_:(0,)*len(shape))
    S=jax.ShapeDtypeStruct
    blk=pl.BlockSpec((rows,256),lambda i,*_:(0,i))
    wcol=lambda j: pl.BlockSpec((D,256),lambda i,*_:(0,3*j+i))
    return pl.pallas_call(kc_kernel,
      grid_spec=pltpu.PrefetchScalarGridSpec(num_scalar_prefetch=1,grid=(3,),
      in_specs=[cst((rows,D))]*5+[blk]*3+[pl.BlockSpec((rows,128),lambda i,*_:(0,i)),cst((rows,128)),cst((rows,128)),
        pl.BlockSpec((256,D),lambda i,*_:(i,0)),wcol(0),wcol(1),wcol(2),cst((8,D))],
      out_specs=[cst((rows,D)),cst((4,4,96,D)),cst((4,4,96,D)),cst((8,D))],
      scratch_shapes=[pltpu.VMEM((rows,D),F32),pltpu.VMEM((rows,D),BF),pltpu.VMEM((D,rows),BF),pltpu.VMEM((rows,D),F32),pltpu.VMEM((D,D),BF),pltpu.VMEM((rows,D),BF)]),
      out_shape=[S((rows,D),BF),S((4,4,96,D),BF),S((4,4,96,D),BF),S((8,D),F32)],
      name="attend_backward",
      cost_estimate=pl.CostEstimate(flops=30_000_000*1000,bytes_accessed=16_000_000,transcendentals=0),
      compiler_params=pltpu.CompilerParams(vmem_limit_bytes=VL),
    )(rel,x,cot,res,dn,att,q,k,v,lse,eq,ek,wo,wi,wi,wi,par)


def on_device(n_dp, n_seq, patches, segments, first_gain, first_bias, input_weight, query_bias, value_bias, output_weight,
              output_bias, second_gain, second_bias, up_weight, up_bias, down_weight, down_bias, cotangent):
    strips, length, D = patches.shape
    dp, z = lax.axis_index("dp"), lax.axis_index("seq")
    core = dp % 2
    stride = n_dp // 8
    both = ("dp", "seq")

    def owned(at_z, at_core):
        k = at_z - at_core
        return k, (0 <= k) & (k < strips)

    def outward(d):
        pairs = []
        for g in range(n_dp):
            for a in range(n_seq):
                b = (a + d) % n_seq
                if owned(b, g % 2)[1]:
                    pairs.append((g * n_seq + a, g * n_seq + b))
        return pairs

    def homeward(d):
        return [(b, a) for a, b in outward(d)]

    def pick(array, d):
        k, fine = owned((z + d) % n_seq, core)
        part = lax.dynamic_index_in_dim(array, jnp.clip(k, 0, strips - 1), 0, keepdims=False)
        return jnp.where(fine, part, jnp.zeros_like(part)) if d == 0 else part

    def gather(array):
        return [pick(array, 0)] + [lax.ppermute(pick(array, d), both, outward(d)) for d in range(1, n_seq)]

    def home(array):
        parts = array.reshape(n_seq, PART, D)
        got = [parts[0]] + [lax.ppermute(parts[d], both, homeward(d)) for d in range(1, n_seq)]
        rows = []
        for k in range(strips):
            at = (k + core - z) % n_seq
            row = got[0]
            for d in range(1, n_seq):
                row = jnp.where(at == d, got[d], row)
            rows.append(row[:length])
        return jnp.stack(rows)

    pad = lambda a: jnp.pad(a, ((0, 0), (0, PART - length), (0, 0)))
    ids = jnp.pad(segments, ((0, 0), (0, PART - length)), constant_values=4).astype(BF)
    ids = jnp.broadcast_to(ids[:, :, None], (strips, PART, 128))
    ids = jnp.concatenate(gather(ids), axis=0)
    lane = lax.broadcasted_iota(jnp.int32, ids.shape, 1)
    same = ids == lane.astype(BF)
    eq = jnp.where(same | (lane >= 5), 0.0, -1e30).astype(BF)
    ek = jnp.where((same & (lane < 5)) | ((lane >= 5) & (lane < 8)), 1.0, 0.0).astype(BF)
    par = jnp.stack([first_gain, first_bias, query_bias, value_bias, output_bias, second_gain, second_bias, down_bias]).astype(F32)
    ub = up_bias.astype(F32).reshape(1, -1)
    x = jnp.concatenate(gather(pad(patches)), axis=0)
    later, _ = lax.optimization_barrier((cotangent, x))
    cot = jnp.concatenate(gather(pad(later)), axis=0)
    rel = jnp.stack([dp // stride, z]).astype(jnp.int32)

    q, k, v, att, lse, nmid, res = ka(x, eq, ek, par, input_weight, output_weight)

    def swap(value, bit):
        return lax.ppermute(value, "dp", [(i, i ^ (stride << bit)) for i in range(n_dp)])

    def add(a, b):
        return (a.astype(F32) + b.astype(F32)).astype(BF)

    def halve(keep, got, bits):
        for n, bit in zip((2, 1), bits):
            sent = add(keep[n:], got[n:])
            kept = add(keep[:n], got[:n])
            keep, got = kept, swap(sent, bit)
        return keep[0].astype(F32) + got[0].astype(F32)

    downs, grads_back = res, par
    ub_grads, ups_parts, downs_parts = [], [], []

    def over_seq(value):
        value_bf = value.astype(BF)
        total = value[0]
        for s in range(1, n_seq):
            total += lax.ppermute(value_bf[s], "seq", [(i, i ^ s) for i in range(n_seq)]).astype(F32)
        return total

    for j in range(3):
        downs, grads_back, keep, send, ubg = kb(j, rel, nmid, cot, up_weight, ub, down_weight, downs, grads_back)
        got = swap(send, 0)
        ups_parts.append(over_seq(halve(keep[0], got[0], (1, 2))))
        downs_parts.append(over_seq(halve(keep[1], got[1], (2, 1))))
        ub_grads.append(ubg)
    block_output = home(downs)
    up_grad = jnp.stack([u.reshape(2, 96, 128) for u in ups_parts])
    up_grad = up_grad.transpose(2, 1, 0, 3).reshape(96, 768)
    down_grad = jnp.stack(downs_parts)
    down_grad = down_grad.transpose(0, 2, 1).reshape(384, 192)
    ub_grad = jnp.stack(ub_grads).reshape(3, 8, 128).transpose(1, 0, 2).reshape(4, D)

    ing, keep, send, vec = kc(rel, x, cot, res, grads_back, att, q, k, v, lse, eq, ek, output_weight, input_weight, par)
    input_grad = home(ing).astype(F32)
    got = swap(send, 0)
    chunk = [halve(keep[c], got[c], (1, 2) if c in (0, 3) else (2, 1)).astype(BF) for c in range(4)]
    in_rows = jnp.concatenate([chunk[i][:, 256 * j:256 * j + 256] for j in range(3) for i in range(3)], axis=1)

    def columns_over_seq(rows):
        width = rows.shape[1] // n_seq
        cut = lambda s: lax.dynamic_slice_in_dim(rows, (z ^ s) * width, width, 1)
        total = cut(0).astype(F32)
        for s in range(1, n_seq):
            total += lax.ppermute(cut(s), "seq", [(i, i ^ s) for i in range(n_seq)]).astype(F32)
        return total

    in_grad = columns_over_seq(in_rows)
    out_grad = columns_over_seq(chunk[3])

    vec = jnp.concatenate([vec, ub_grad], axis=0)
    bit = 1
    while bit < n_dp:
        vec += lax.ppermute(vec, "dp", [(i, i ^ bit) for i in range(n_dp)])
        bit *= 2
    bit = 1
    while bit < n_seq:
        vec += lax.ppermute(vec, "seq", [(i, i ^ bit) for i in range(n_seq)])
        bit *= 2

    weights = [in_grad, out_grad, up_grad, down_grad]
    if stride > 1:
        groups = [[g * stride + t for t in range(stride)] for g in range(8)]
        weights = [lax.psum_scatter(w, "dp", scatter_dimension=0, axis_index_groups=groups, tiled=True) for w in weights]
    in_grad, out_grad, up_grad, down_grad = weights
    return (block_output, input_grad, vec[0], vec[1], in_grad, vec[2], vec[3], out_grad, vec[4], vec[5], vec[6], up_grad,
            vec[8:12].reshape(-1), down_grad, vec[7])


def solution(mesh):
    rep = P()
    rows = P("dp", "seq", None)
    cut = P("dp", "seq")
    return jax.shard_map(
        functools.partial(on_device, mesh.shape["dp"], mesh.shape["seq"]),
        mesh=mesh,
        in_specs=(rows, cut) + (rep,) * 13 + (rows,),
        out_specs=(rows, rows, rep, rep, cut, rep, rep, cut, rep, rep, rep, cut, rep, cut, rep),
        check_vma=False,
    )
```

time: 762 us -> 302 us (0.40)
  waiting for transfers between devices: 302 us -> 66.3 us
  local copies, waits for them, and re-layouts: 138 us -> 6.48 us
  blocking collectives: 128 us -> 0 us
  matrix products: 110 us -> 0 us
  starting transfers between devices: 20.8 us -> 115 us
  Pallas kernels: 0 us -> 88.5 us
  other arithmetic: 41.3 us -> 18.1 us
  between operations: 14.9 us -> 1.98 us
    reduce_scatter x5 -> x0, waiting for transfers between devices: 205 us -> none  [the longest x1 77.4 us: on_device(): lax.psum_scatter(up_weight_grad, 'dp', scatter_dimension=0, tiled=True)]
    ppermute x0 -> x68, starting transfers between devices: none -> 115 us  [the longest x6 25.8 us: home(): lax.ppermute(parts[d], both, homeward(d))]
    dot_general x33 -> x0, matrix products: 110 us -> none  [the longest x4 24.9 us: column_sum(): lax.dot_general(left, right, (((0,), (0,)), ((), ())), preferred_element_...]
    pallas_call x0 -> x5, Pallas kernels: none -> 88.5 us  [the longest x3 40.7 us: kb(): pl.pallas_call(functools.partial(kb_kernel, sb, first, last), grid_spec=p...]
    all_gather x1 -> x0, blocking collectives: 84.5 us -> none  [on_device(): whole_ids = lax.all_gather(segments, 'seq', axis=1, tiled=True)]
    ppermute x0 -> x68, waiting for transfers between devices: none -> 66.3 us  [the longest x24 33.4 us: swap(): lax.ppermute(value, 'dp', [(i, i ^ stride << bit) for i in range(n_dp)])]
    all_to_all x4 -> x0, waiting for transfers between devices: 66 us -> none  [the longest x1 37.1 us: on_device(): lax.all_to_all(grad_mixed, 'seq', split_axis=1, concat_axis=3, tiled=True)]
    psum x1 -> x0, blocking collectives: 43.6 us -> none  [on_device(): lax.psum((first_gain_grad, first_bias_grad, query_bias_grad, value_bias_g...]
  transfers between devices with their start and end apart: 12 -> 68, of which waited for: 8 -> 28; matrix products, arithmetic and copies ran while one was open for 21% -> 6% of each run, Pallas kernels for 0% -> 6%
where the time goes in v1:
time: 302 us; the launch traced here: 296 us
  starting transfers between devices  115 us (38%)
  Pallas kernels  88.5 us (29%)
  waiting for transfers between devices  66.3 us (22%)
  other arithmetic  18.1 us (6%)
  local copies, waits for them, and re-layouts  6.48 us (2%)
    pallas_call x3, Pallas kernels, kb(): pl.pallas_call(functools.partial(kb_kernel, sb, first, last), grid_spec=p...  40.7 us
    ppermute x24, waiting for transfers between devices, swap(): lax.ppermute(value, 'dp', [(i, i ^ stride << bit) for i in range(n_dp)])  33.4 us
    pallas_call x1, Pallas kernels, kc(): pl.pallas_call(kc_kernel, grid_spec=pltpu.PrefetchScalarGridSpec(num_scal...  30.1 us
    ppermute x6, starting transfers between devices, home(): lax.ppermute(parts[d], both, homeward(d))  25.8 us
    ppermute x24, starting transfers between devices, swap(): lax.ppermute(value, 'dp', [(i, i ^ stride << bit) for i in range(n_dp)])  25.3 us
    ppermute x18, starting transfers between devices, over_seq(): lax.ppermute(value_bf[s], 'seq', [(i, i ^ s) for i in range(n_seq)])  24.4 us
    ppermute x9, starting transfers between devices, gather(): lax.ppermute(pick(array, d), both, outward(d))  24.1 us
    pallas_call x1, Pallas kernels, ka(): pl.pallas_call(ka_kernel, grid=(n,), in_specs=[full(x), full(eq), full(ek...  17.7 us
  transfers between devices with their start and end apart: 68, of which 28 were waited for; matrix products, arithmetic and copies ran while one was open for 6% of the time, Pallas kernels for 6%

profile of v1, /device:TPU:0, one launch (start us, length us, event | category | flops | bytes accessed | tf_op | source)
XLA Modules:
  0.0 296.4 jit_solution(18428159613062727484)
XLA Ops:
  2.2 4.9 %collective-permute-start = (bf16[136,768]{1,0:T(8,128)(2,1)S(1)}, bf16[136,768]{1,0:T(8,128)(2,1)S(1)}, u32[]{:S(2)}, u32[]{:S(2)}) collective-permute-start(bf16[136,768]{1,0:T(8,128)(2,1)S(1)} %get-tuple-element.132), channel_id=1, source_target_pairs={{0,1},{1,2},{3,0},{4,5},{5,6},{6,7},{8,9},{9,10},{11,8},{12,13},{1... | collective-permute-start | bytes 626696 | tf_op jit(solution)/shard_map/ppermute | solution.py:301
  10.3 2.5 collective-permute-start.3
  12.8 3.3 %collective-permute-start.4 = (bf16[136,128]{1,0:T(8,128)(2,1)S(1)}, bf16[136,128]{1,0:T(8,128)(2,1)S(1)}, u32[]{:S(2)}, u32[]{:S(2)}) collective-permute-start(bf16[136,128]{1,0:T(8,128)(2,1)S(1)} %broadcast_in_dim.38), channel_id=1, source_target_pairs={{0,2},{2,0},{3,1},{4,6},{5,7},{7,5},{8,10},{10,8},{11,9},{12,14},{... | collective-permute-start | bytes 104456 | tf_op jit(solution)/shard_map/ppermute | solution.py:301
  23.5 4.3 %collective-permute-done.2 = bf16[136,768]{1,0:T(8,128)(2,1)S(1)} collective-permute-done((bf16[136,768]{1,0:T(8,128)(2,1)S(1)}, bf16[136,768]{1,0:T(8,128)(2,1)S(1)}, u32[]{:S(2)}, u32[]{:S(2)}) %collective-permute-start.2) | collective-permute-done | bytes 208928 | tf_op jit(solution)/shard_map/ppermute | solution.py:301
  28.9 5.2 %collective-permute-start.6 = (bf16[136,768]{1,0:T(8,128)(2,1)S(1)}, bf16[136,768]{1,0:T(8,128)(2,1)S(1)}, u32[]{:S(2)}, u32[]{:S(2)}) collective-permute-start(bf16[136,768]{1,0:T(8,128)(2,1)S(1)} %get-tuple-element.128), channel_id=1, source_target_pairs={{0,1},{1,2},{3,0},{4,5},{5,6},{6,7},{8,9},{9,10},{11,8},{12,13},{1... | collective-permute-start | bytes 626696 | tf_op jit(solution)/shard_map/ppermute | solution.py:301
  37.5 17.7 %attend_forward.1 = (bf16[544,768]{1,0:T(8,128)(2,1)}, bf16[544,768]{1,0:T(8,128)(2,1)}, bf16[544,768]{1,0:T(8,128)(2,1)}, bf16[544,768]{1,0:T(8,128)(2,1)}, f32...) custom-call(bf16[544,768]{1,0:T(8,128)(2,1)} %pad_maximum_fusion.x_ref, ...), custom_call_target="tpu_custom_call" | custom-call | flops 16999999488 | bytes 12000000 | tf_op jit(solution)/shard_map/attend_forward/pallas_call | solution.py:84
  56.2 13.1 %feed_forward.3 = (f32[544,768]{1,0:T(8,128)}, f32[544,768]{1,0:T(8,128)}, bf16[2,4,4,192,128]{4,3,2,1,0:T(8,128)(2,1)}, bf16[2,4,4,192,128]{4,3,2,1,0:T(8,128)(2,1)}, f32[1,1024]{1,0:T(1,128)}) custom-call(s32[2]{0:T(128)} %pad_add_fusion.rel_ref, bf16[544,768]{1,0:T(8,128)(2,1)} %get-tuple-element.42.nmid_ref, bf16[544,768]{1,0:T(8,128)(2,1)} %pad_maximum_fusion.1.cot_ref, ...), custom_call_target="tpu_custom_call" | custom-call | flops 14000000000 | bytes 16000000 | tf_op jit(solution)/shard_map/feed_forward/pallas_call | solution.py:166
  69.4 14.2 %feed_forward.4 = (f32[544,768]{1,0:T(8,128)}, f32[544,768]{1,0:T(8,128)}, bf16[2,4,4,192,128]{4,3,2,1,0:T(8,128)(2,1)}, bf16[2,4,4,192,128]{4,3,2,1,0:T(8,128)(2,1)}, f32[1,1024]{1,0:T(1,128)}) custom-call(s32[2]{0:T(128)} %pad_add_fusion.rel_ref, bf16[544,768]{1,0:T(8,128)(2,1)} %get-tuple-element.42.nmid_ref, bf16[544,768]{1,0:T(8,128)(2,1)} %pad_maximum_fusion.1.cot_ref, ...), custom_call_target="tpu_custom_call" | custom-call | flops 14000000000 | bytes 16000000 | tf_op jit(solution)/shard_map/feed_forward/pallas_call | solution.py:166
  83.6 13.4 %feed_forward.5 = (bf16[544,768]{1,0:T(8,128)(2,1)}, f32[544,768]{1,0:T(8,128)}, bf16[2,4,4,192,128]{4,3,2,1,0:T(8,128)(2,1)}, bf16[2,4,4,192,128]{4,3,2,1,0:T(8,128)(2,1)}, f32[1,1024]{1,0:T(1,128)}) custom-call(s32[2]{0:T(128)} %pad_add_fusion.rel_ref, bf16[544,768]{1,0:T(8,128)(2,1)} %get-tuple-element.42.nmid_ref, ...), custom_call_target="tpu_custom_call" | custom-call | flops 14000000000 | bytes 16000000 | tf_op jit(solution)/shard_map/feed_forward/pallas_call | solution.py:166
  97.7 30.1 %attend_backward.1 = (bf16[544,768]{1,0:T(8,128)(2,1)}, bf16[4,4,96,768]{3,2,1,0:T(8,128)(2,1)}, bf16[4,4,96,768]{3,2,1,0:T(8,128)(2,1)}, f32[8,768]{1,0:T(8,128)}) custom-call(s32[2]{0:T(128)} %pad_add_fusion.rel_ref, bf16[544,768]{1,0:T(8,128)(2,1)} %pad_maximum_fusion.x_ref, bf16[544,768]{1,0:T(8,128)(2,1)} %pad_maximum_fusion.1.cot_ref, ...), custom_call_target="tpu_custom_call" | custom-call | flops 30000001024 | bytes 16000000 | tf_op jit(solution)/shard_map/attend_backward/pallas_call | solution.py:258
  128.6 3.4 %collective-permute-start.15 = (f32[12,768]{1,0:T(8,128)S(1)}, f32[12,768]{1,0:T(8,128)S(1)}, u32[]{:S(2)}, u32[]{:S(2)}) collective-permute-start(f32[12,768]{1,0:T(8,128)S(1)} %constant_dynamic-update-slice_fusion), channel_id=1, source_target_pairs={{0,4},{4,0},{8,12},{12,8},{16,20},{20,16},{24,28},{28,24},{1,5},{5... | collective-permute-start | bytes 110600 | tf_op jit(solution)/shard_map/ppermute | solution.py:388
  134.5 2.6 collective-permute-done.16
  138.7 2.6 collective-permute-done.17
  142.2 4.2 %collective-permute-start.10 = (bf16[136,768]{1,0:T(8,128)(2,1)}, bf16[136,768]{1,0:T(8,128)(2,1)S(1)}, u32[]{:S(2)}, u32[]{:S(2)}) collective-permute-start(bf16[136,768]{1,0:T(8,128)(2,1)} %get-tuple-element.125), channel_id=1, source_target_pairs={{2,0},{0,2},{1,3},{6,4},{7,5},{5,7},{10,8},{8,10},{9,11},{14,12},{... | collective-permute-start | bytes 626696 | tf_op jit(solution)/shard_map/ppermute | solution.py:305
  148.3 3.9 %collective-permute-start.9 = (bf16[136,768]{1,0:T(8,128)(2,1)}, bf16[136,768]{1,0:T(8,128)(2,1)S(1)}, u32[]{:S(2)}, u32[]{:S(2)}) collective-permute-start(bf16[136,768]{1,0:T(8,128)(2,1)} %get-tuple-element.126), channel_id=1, source_target_pairs={{0,1},{1,2},{2,3},{7,4},{5,6},{6,7},{8,9},{9,10},{10,11},{15,12},{... | collective-permute-start | bytes 626696 | tf_op jit(solution)/shard_map/ppermute | solution.py:305
  153.2 8.2 %collective-permute-done.19 = f32[12,768]{1,0:T(8,128)S(1)} collective-permute-done((f32[12,768]{1,0:T(8,128)S(1)}, f32[12,768]{1,0:T(8,128)S(1)}, u32[]{:S(2)}, u32[]{:S(2)}) %collective-permute-start.19) | collective-permute-done | bytes 36896 | tf_op jit(solution)/shard_map/ppermute | solution.py:392
  164.7 5.3 %collective-permute-start.13 = (bf16[136,768]{1,0:T(8,128)(2,1)}, bf16[136,768]{1,0:T(8,128)(2,1)S(1)}, u32[]{:S(2)}, u32[]{:S(2)}) collective-permute-start(bf16[136,768]{1,0:T(8,128)(2,1)} %get-tuple-element.119), channel_id=1, source_target_pairs={{2,0},{0,2},{1,3},{6,4},{7,5},{5,7},{10,8},{8,10},{9,11},{14,12},{... | collective-permute-start | bytes 626696 | tf_op jit(solution)/shard_map/ppermute | solution.py:305
  170.1 8.9 %collective-permute-start.14 = (bf16[136,768]{1,0:T(8,128)(2,1)}, bf16[136,768]{1,0:T(8,128)(2,1)S(1)}, u32[]{:S(2)}, u32[]{:S(2)}) collective-permute-start(bf16[136,768]{1,0:T(8,128)(2,1)} %get-tuple-element.117), channel_id=1, source_target_pairs={{1,0},{2,1},{0,3},{5,4},{6,5},{7,6},{9,8},{10,9},{8,11},{13,12},{1... | collective-permute-start | bytes 626696 | tf_op jit(solution)/shard_map/ppermute | solution.py:305
  180.0 3.1 %collective-permute-done.14 = bf16[136,768]{1,0:T(8,128)(2,1)S(1)} collective-permute-done((bf16[136,768]{1,0:T(8,128)(2,1)}, bf16[136,768]{1,0:T(8,128)(2,1)S(1)}, u32[]{:S(2)}, u32[]{:S(2)}) %collective-permute-start.14) | collective-permute-done | bytes 208928 | tf_op jit(solution)/shard_map/ppermute | solution.py:305
  193.3 4.3 %collective-permute-done.53 = bf16[2,4,192,128]{3,2,1,0:T(8,128)(2,1)S(1)} collective-permute-done((bf16[2,4,192,128]{3,2,1,0:T(8,128)(2,1)S(1)}, bf16[2,4,192,128]{3,2,1,0:T(8,128)(2,1)S(1)}, u32[]{:S(2)}, u32[]{:S(2)}) %collective-permute-start.53) | collective-permute-done | bytes 393248 | tf_op jit(solution)/shard_map/ppermute | solution.py:333
  199.1 6.9 %collective-permute-done.58 = bf16[2,4,192,128]{3,2,1,0:T(8,128)(2,1)S(1)} collective-permute-done((bf16[2,4,192,128]{3,2,1,0:T(8,128)(2,1)S(1)}, bf16[2,4,192,128]{3,2,1,0:T(8,128)(2,1)S(1)}, u32[]{:S(2)}, u32[]{:S(2)}) %collective-permute-start.58) | collective-permute-done | bytes 393248 | tf_op jit(solution)/shard_map/ppermute | solution.py:333
  207.6 6.1 %collective-permute-done.63 = bf16[2,4,192,128]{3,2,1,0:T(8,128)(2,1)S(1)} collective-permute-done((bf16[2,4,192,128]{3,2,1,0:T(8,128)(2,1)S(1)}, bf16[2,4,192,128]{3,2,1,0:T(8,128)(2,1)S(1)}, u32[]{:S(2)}, u32[]{:S(2)}) %collective-permute-start.63) | collective-permute-done | bytes 393248 | tf_op jit(solution)/shard_map/ppermute | solution.py:333
  217.5 3.2 %collective-permute-done.48 = bf16[2,4,192,128]{3,2,1,0:T(8,128)(2,1)S(1)} collective-permute-done((bf16[2,4,192,128]{3,2,1,0:T(8,128)(2,1)S(1)}, bf16[2,4,192,128]{3,2,1,0:T(8,128)(2,1)S(1)}, u32[]{:S(2)}, u32[]{:S(2)}) %collective-permute-start.48) | collective-permute-done | bytes 393248 | tf_op jit(solution)/shard_map/ppermute | solution.py:333
  221.5 3.4 %collective-permute-done.54 = bf16[1,4,192,128]{3,2,1,0:T(8,128)(2,1)S(1)} collective-permute-done((bf16[1,4,192,128]{3,2,1,0:T(8,128)(2,1)S(1)}, bf16[1,4,192,128]{3,2,1,0:T(8,128)(2,1)S(1)}, u32[]{:S(2)}, u32[]{:S(2)}) %collective-permute-start.54) | collective-permute-done | bytes 196640 | tf_op jit(solution)/shard_map/ppermute | solution.py:333
  225.8 3.3 %collective-permute-done.59 = bf16[1,4,192,128]{3,2,1,0:T(8,128)(2,1)S(1)} collective-permute-done((bf16[1,4,192,128]{3,2,1,0:T(8,128)(2,1)S(1)}, bf16[1,4,192,128]{3,2,1,0:T(8,128)(2,1)S(1)}, u32[]{:S(2)}, u32[]{:S(2)}) %collective-permute-start.59) | collective-permute-done | bytes 196640 | tf_op jit(solution)/shard_map/ppermute | solution.py:333
  232.5 3.8 %collective-permute-start.57 = (bf16[192,128]{1,0:T(8,128)(2,1)S(1)}, bf16[192,128]{1,0:T(8,128)(2,1)S(1)}, u32[]{:S(2)}, u32[]{:S(2)}) collective-permute-start(bf16[192,128]{1,0:T(8,128)(2,1)S(1)} %get-tuple-element.139), channel_id=1, source_target_pairs={{0,3},{1,2},{2,1},{3,0},{4,7},{5,6},{6,5},{7,4},{8,11},{9,10},{10,... | collective-permute-start | bytes 147464 | tf_op jit(solution)/shard_map/ppermute | solution.py:352
  237.4 3.7 %collective-permute-start.62 = (bf16[192,128]{1,0:T(8,128)(2,1)S(1)}, bf16[192,128]{1,0:T(8,128)(2,1)S(1)}, u32[]{:S(2)}, u32[]{:S(2)}) collective-permute-start(bf16[192,128]{1,0:T(8,128)(2,1)S(1)} %get-tuple-element.142), channel_id=1, source_target_pairs={{0,3},{1,2},{2,1},{3,0},{4,7},{5,6},{6,5},{7,4},{8,11},{9,10},{10,... | collective-permute-start | bytes 147464 | tf_op jit(solution)/shard_map/ppermute | solution.py:352
  243.0 2.6 collective-permute-start.67
  255.6 3.1 %collective-permute-start.51 = (bf16[192,128]{1,0:T(8,128)(2,1)S(1)}, bf16[192,128]{1,0:T(8,128)(2,1)S(1)}, u32[]{:S(2)}, u32[]{:S(2)}) collective-permute-start(bf16[192,128]{1,0:T(8,128)(2,1)S(1)} %get-tuple-element.155), channel_id=1, source_target_pairs={{0,2},{1,3},{2,0},{3,1},{4,6},{5,7},{6,4},{7,5},{8,10},{9,11},{10,... | collective-permute-start | bytes 147464 | tf_op jit(solution)/shard_map/ppermute | solution.py:352
  274.0 2.7 collective-permute-done.23
  285.7 2.9 collective-permute-start.28
  292.1 3.3 %collective-permute-done.29 = bf16[96,576]{1,0:T(8,128)(2,1)S(1)} collective-permute-done((bf16[96,576]{1,0:T(8,128)(2,1)S(1)}, bf16[96,576]{1,0:T(8,128)(2,1)S(1)}, u32[]{:S(2)}, u32[]{:S(2)}) %collective-permute-start.29) | collective-permute-done | bytes 110624 | tf_op jit(solution)/shard_map/ppermute | solution.py:379
  (249 shorter events, 94.3 us)
Async XLA Ops:
  2.2 21.4 %collective-permute-start = (bf16[136,768]{1,0:T(8,128)(2,1)S(1)}, bf16[136,768]{1,0:T(8,128)(2,1)S(1)}, u32[]{:S(2)}, u32[]{:S(2)}) collective-permute-start(bf16[136,768]{1,0:T(8,128)(2,1)S(1)} %get-tuple-element.132), channel_id=1, source_target_pairs={{0,1},{1,2},{3,0},{4,5},{5,6},{6,7},{8,9},{9,10},{11,8},{12,13},{1... | collective-permute-start | bytes 626696 | tf_op jit(solution)/shard_map/ppermute | solution.py:301
  7.1 16.4 %collective-permute-start.1 = (bf16[136,768]{1,0:T(8,128)(2,1)S(1)}, bf16[136,768]{1,0:T(8,128)(2,1)S(1)}, u32[]{:S(2)}, u32[]{:S(2)}) collective-permute-start(bf16[136,768]{1,0:T(8,128)(2,1)S(1)} %get-tuple-element.133), channel_id=1, source_target_pairs={{0,2},{2,0},{3,1},{4,6},{5,7},{7,5},{8,10},{10,8},{11,9},{12,14},{... | collective-permute-start | bytes 626696 | tf_op jit(solution)/shard_map/ppermute | solution.py:301
  10.3 9.3 %collective-permute-start.3 = (bf16[136,128]{1,0:T(8,128)(2,1)S(1)}, bf16[136,128]{1,0:T(8,128)(2,1)S(1)}, u32[]{:S(2)}, u32[]{:S(2)}) collective-permute-start(bf16[136,128]{1,0:T(8,128)(2,1)S(1)} %broadcast_in_dim.36), channel_id=1, source_target_pairs={{0,1},{1,2},{3,0},{4,5},{5,6},{6,7},{8,9},{9,10},{11,8},{12,13},{1... | collective-permute-start | bytes 104456 | tf_op jit(solution)/shard_map/ppermute | solution.py:301
  28.9 26.3 %collective-permute-start.6 = (bf16[136,768]{1,0:T(8,128)(2,1)S(1)}, bf16[136,768]{1,0:T(8,128)(2,1)S(1)}, u32[]{:S(2)}, u32[]{:S(2)}) collective-permute-start(bf16[136,768]{1,0:T(8,128)(2,1)S(1)} %get-tuple-element.128), channel_id=1, source_target_pairs={{0,1},{1,2},{3,0},{4,5},{5,6},{6,7},{8,9},{9,10},{11,8},{12,13},{1... | collective-permute-start | bytes 626696 | tf_op jit(solution)/shard_map/ppermute | solution.py:301
  34.1 21.2 %collective-permute-start.7 = (bf16[136,768]{1,0:T(8,128)(2,1)S(1)}, bf16[136,768]{1,0:T(8,128)(2,1)S(1)}, u32[]{:S(2)}, u32[]{:S(2)}) collective-permute-start(bf16[136,768]{1,0:T(8,128)(2,1)S(1)} %get-tuple-element.129), channel_id=1, source_target_pairs={{0,2},{2,0},{3,1},{4,6},{5,7},{7,5},{8,10},{10,8},{11,9},{12,14},{... | collective-permute-start | bytes 626696 | tf_op jit(solution)/shard_map/ppermute | solution.py:301
  36.2 19.1 %collective-permute-start.8 = (bf16[136,768]{1,0:T(8,128)(2,1)S(1)}, bf16[136,768]{1,0:T(8,128)(2,1)S(1)}, u32[]{:S(2)}, u32[]{:S(2)}) collective-permute-start(bf16[136,768]{1,0:T(8,128)(2,1)S(1)} %get-tuple-element.130), channel_id=1, source_target_pairs={{1,0},{2,1},{3,2},{4,7},{6,5},{7,6},{9,8},{10,9},{11,10},{12,15},{... | collective-permute-start | bytes 626696 | tf_op jit(solution)/shard_map/ppermute | solution.py:301
  138.7 45.7 %collective-permute-start.35 = (bf16[2,4,4,192,128]{4,3,2,1,0:T(8,128)(2,1)}, bf16[2,4,4,192,128]{4,3,2,1,0:T(8,128)(2,1)S(1)}, u32[]{:S(2)}, u32[]{:S(2)}) collective-permute-start(bf16[2,4,4,192,128]{4,3,2,1,0:T(8,128)(2,1)} %get-tuple-element.64), channel_id=1, source_target_pairs={{0,4},{4,0},{8,12},{12,8},{16,20},{20,16},{24,28},{28,24},{1,5},{5... | collective-permute-start | bytes 4718600 | tf_op jit(solution)/shard_map/ppermute | solution.py:333
  141.2 11.0 %collective-permute-start.18 = (f32[12,768]{1,0:T(8,128)S(1)}, f32[12,768]{1,0:T(8,128)S(1)}, u32[]{:S(2)}, u32[]{:S(2)}) collective-permute-start(f32[12,768]{1,0:T(8,128)S(1)} %add.386), channel_id=1, source_target_pairs={{0,1},{1,0},{2,3},{3,2},{4,5},{5,4},{6,7},{7,6},{8,9},{9,8},{10,11... | collective-permute-start | bytes 110600 | tf_op jit(solution)/shard_map/ppermute | solution.py:392
  142.2 20.6 %collective-permute-start.10 = (bf16[136,768]{1,0:T(8,128)(2,1)}, bf16[136,768]{1,0:T(8,128)(2,1)S(1)}, u32[]{:S(2)}, u32[]{:S(2)}) collective-permute-start(bf16[136,768]{1,0:T(8,128)(2,1)} %get-tuple-element.125), channel_id=1, source_target_pairs={{2,0},{0,2},{1,3},{6,4},{7,5},{5,7},{10,8},{8,10},{9,11},{14,12},{... | collective-permute-start | bytes 626696 | tf_op jit(solution)/shard_map/ppermute | solution.py:305
  146.4 16.8 %collective-permute-start.11 = (bf16[136,768]{1,0:T(8,128)(2,1)}, bf16[136,768]{1,0:T(8,128)(2,1)S(1)}, u32[]{:S(2)}, u32[]{:S(2)}) collective-permute-start(bf16[136,768]{1,0:T(8,128)(2,1)} %get-tuple-element.123), channel_id=1, source_target_pairs={{1,0},{2,1},{0,3},{5,4},{6,5},{7,6},{9,8},{10,9},{8,11},{13,12},{1... | collective-permute-start | bytes 626696 | tf_op jit(solution)/shard_map/ppermute | solution.py:305
  148.3 16.4 %collective-permute-start.9 = (bf16[136,768]{1,0:T(8,128)(2,1)}, bf16[136,768]{1,0:T(8,128)(2,1)S(1)}, u32[]{:S(2)}, u32[]{:S(2)}) collective-permute-start(bf16[136,768]{1,0:T(8,128)(2,1)} %get-tuple-element.126), channel_id=1, source_target_pairs={{0,1},{1,2},{2,3},{7,4},{5,6},{6,7},{8,9},{9,10},{10,11},{15,12},{... | collective-permute-start | bytes 626696 | tf_op jit(solution)/shard_map/ppermute | solution.py:305
  152.3 9.1 %collective-permute-start.19 = (f32[12,768]{1,0:T(8,128)S(1)}, f32[12,768]{1,0:T(8,128)S(1)}, u32[]{:S(2)}, u32[]{:S(2)}) collective-permute-start(f32[12,768]{1,0:T(8,128)S(1)} %add.387), channel_id=1, source_target_pairs={{0,2},{1,3},{2,0},{3,1},{4,6},{5,7},{6,4},{7,5},{8,10},{9,11},{10,... | collective-permute-start | bytes 110600 | tf_op jit(solution)/shard_map/ppermute | solution.py:392
  161.4 25.7 %collective-permute-start.41 = (bf16[2,4,4,192,128]{4,3,2,1,0:T(8,128)(2,1)}, bf16[2,4,4,192,128]{4,3,2,1,0:T(8,128)(2,1)}, u32[]{:S(2)}, u32[]{:S(2)}) collective-permute-start(bf16[2,4,4,192,128]{4,3,2,1,0:T(8,128)(2,1)} %get-tuple-element.66), channel_id=1, source_target_pairs={{0,4},{4,0},{8,12},{12,8},{16,20},{20,16},{24,28},{28,24},{1,5},{5... | collective-permute-start | bytes 4718600 | tf_op jit(solution)/shard_map/ppermute | solution.py:333
  162.7 27.2 %collective-permute-start.47 = (bf16[2,4,4,192,128]{4,3,2,1,0:T(8,128)(2,1)}, bf16[2,4,4,192,128]{4,3,2,1,0:T(8,128)(2,1)S(1)}, u32[]{:S(2)}, u32[]{:S(2)}) collective-permute-start(bf16[2,4,4,192,128]{4,3,2,1,0:T(8,128)(2,1)} %get-tuple-element.68), channel_id=1, source_target_pairs={{0,4},{4,0},{8,12},{12,8},{16,20},{20,16},{24,28},{28,24},{1,5},{5... | collective-permute-start | bytes 4718600 | tf_op jit(solution)/shard_map/ppermute | solution.py:333
  164.7 15.3 %collective-permute-start.13 = (bf16[136,768]{1,0:T(8,128)(2,1)}, bf16[136,768]{1,0:T(8,128)(2,1)S(1)}, u32[]{:S(2)}, u32[]{:S(2)}) collective-permute-start(bf16[136,768]{1,0:T(8,128)(2,1)} %get-tuple-element.119), channel_id=1, source_target_pairs={{2,0},{0,2},{1,3},{6,4},{7,5},{5,7},{10,8},{8,10},{9,11},{14,12},{... | collective-permute-start | bytes 626696 | tf_op jit(solution)/shard_map/ppermute | solution.py:305
  170.1 13.0 %collective-permute-start.14 = (bf16[136,768]{1,0:T(8,128)(2,1)}, bf16[136,768]{1,0:T(8,128)(2,1)S(1)}, u32[]{:S(2)}, u32[]{:S(2)}) collective-permute-start(bf16[136,768]{1,0:T(8,128)(2,1)} %get-tuple-element.117), channel_id=1, source_target_pairs={{1,0},{2,1},{0,3},{5,4},{6,5},{7,6},{9,8},{10,9},{8,11},{13,12},{1... | collective-permute-start | bytes 626696 | tf_op jit(solution)/shard_map/ppermute | solution.py:305
  180.0 80.2 %collective-permute-start.20 = (bf16[4,4,96,768]{3,2,1,0:T(8,128)(2,1)S(1)}, bf16[4,4,96,768]{3,2,1,0:T(8,128)(2,1)S(1)}, u32[]{:S(2)}, u32[]{:S(2)}) collective-permute-start(bf16[4,4,96,768]{3,2,1,0:T(8,128)(2,1)S(1)} %copy-done.18), channel_id=1, source_target_pairs={{0,4},{4,0},{8,12},{12,8},{16,20},{20,16},{24,28},{28,24},{1,5},{5... | collective-permute-start | bytes 7077896 | tf_op jit(solution)/shard_map/ppermute | solution.py:333
  185.6 12.0 %collective-permute-start.53 = (bf16[2,4,192,128]{3,2,1,0:T(8,128)(2,1)S(1)}, bf16[2,4,192,128]{3,2,1,0:T(8,128)(2,1)S(1)}, u32[]{:S(2)}, u32[]{:S(2)}) collective-permute-start(bf16[2,4,192,128]{3,2,1,0:T(8,128)(2,1)S(1)} %get-tuple-element.104), channel_id=1, source_target_pairs={{0,16},{4,20},{8,24},{12,28},{16,0},{20,4},{24,8},{28,12},{1,17},{... | collective-permute-start | bytes 1179656 | tf_op jit(solution)/shard_map/ppermute | solution.py:333
  189.1 16.9 %collective-permute-start.58 = (bf16[2,4,192,128]{3,2,1,0:T(8,128)(2,1)S(1)}, bf16[2,4,192,128]{3,2,1,0:T(8,128)(2,1)S(1)}, u32[]{:S(2)}, u32[]{:S(2)}) collective-permute-start(bf16[2,4,192,128]{3,2,1,0:T(8,128)(2,1)S(1)} %get-tuple-element.108), channel_id=1, source_target_pairs={{0,16},{4,20},{8,24},{12,28},{16,0},{20,4},{24,8},{28,12},{1,17},{... | collective-permute-start | bytes 1179656 | tf_op jit(solution)/shard_map/ppermute | solution.py:333
  190.5 23.1 %collective-permute-start.63 = (bf16[2,4,192,128]{3,2,1,0:T(8,128)(2,1)S(1)}, bf16[2,4,192,128]{3,2,1,0:T(8,128)(2,1)S(1)}, u32[]{:S(2)}, u32[]{:S(2)}) collective-permute-start(bf16[2,4,192,128]{3,2,1,0:T(8,128)(2,1)S(1)} %get-tuple-element.112), channel_id=1, source_target_pairs={{0,16},{4,20},{8,24},{12,28},{16,0},{20,4},{24,8},{28,12},{1,17},{... | collective-permute-start | bytes 1179656 | tf_op jit(solution)/shard_map/ppermute | solution.py:333
  191.8 23.4 %collective-permute-start.36 = (bf16[2,4,192,128]{3,2,1,0:T(8,128)(2,1)S(1)}, bf16[2,4,192,128]{3,2,1,0:T(8,128)(2,1)S(1)}, u32[]{:S(2)}, u32[]{:S(2)}) collective-permute-start(bf16[2,4,192,128]{3,2,1,0:T(8,128)(2,1)S(1)} %get-tuple-element.105), channel_id=1, source_target_pairs={{0,8},{4,12},{8,0},{12,4},{16,24},{20,28},{24,16},{28,20},{1,9},{5... | collective-permute-start | bytes 1179656 | tf_op jit(solution)/shard_map/ppermute | solution.py:333
  197.6 18.2 %collective-permute-start.42 = (bf16[2,4,192,128]{3,2,1,0:T(8,128)(2,1)S(1)}, bf16[2,4,192,128]{3,2,1,0:T(8,128)(2,1)S(1)}, u32[]{:S(2)}, u32[]{:S(2)}) collective-permute-start(bf16[2,4,192,128]{3,2,1,0:T(8,128)(2,1)S(1)} %get-tuple-element.109), channel_id=1, source_target_pairs={{0,8},{4,12},{8,0},{12,4},{16,24},{20,28},{24,16},{28,20},{1,9},{5... | collective-permute-start | bytes 1179656 | tf_op jit(solution)/shard_map/ppermute | solution.py:333
  206.0 14.7 %collective-permute-start.48 = (bf16[2,4,192,128]{3,2,1,0:T(8,128)(2,1)S(1)}, bf16[2,4,192,128]{3,2,1,0:T(8,128)(2,1)S(1)}, u32[]{:S(2)}, u32[]{:S(2)}) collective-permute-start(bf16[2,4,192,128]{3,2,1,0:T(8,128)(2,1)S(1)} %get-tuple-element.113), channel_id=1, source_target_pairs={{0,8},{4,12},{8,0},{12,4},{16,24},{20,28},{24,16},{28,20},{1,9},{5... | collective-permute-start | bytes 1179656 | tf_op jit(solution)/shard_map/ppermute | solution.py:333
  213.6 11.3 %collective-permute-start.54 = (bf16[1,4,192,128]{3,2,1,0:T(8,128)(2,1)S(1)}, bf16[1,4,192,128]{3,2,1,0:T(8,128)(2,1)S(1)}, u32[]{:S(2)}, u32[]{:S(2)}) collective-permute-start(bf16[1,4,192,128]{3,2,1,0:T(8,128)(2,1)S(1)} %fusion.10), channel_id=1, source_target_pairs={{0,8},{4,12},{8,0},{12,4},{16,24},{20,28},{24,16},{28,20},{1,9},{5... | collective-permute-start | bytes 589832 | tf_op jit(solution)/shard_map/ppermute | solution.py:333
  215.2 13.9 %collective-permute-start.59 = (bf16[1,4,192,128]{3,2,1,0:T(8,128)(2,1)S(1)}, bf16[1,4,192,128]{3,2,1,0:T(8,128)(2,1)S(1)}, u32[]{:S(2)}, u32[]{:S(2)}) collective-permute-start(bf16[1,4,192,128]{3,2,1,0:T(8,128)(2,1)S(1)} %fusion.8), channel_id=1, source_target_pairs={{0,8},{4,12},{8,0},{12,4},{16,24},{20,28},{24,16},{28,20},{1,9},{5... | collective-permute-start | bytes 589832 | tf_op jit(solution)/shard_map/ppermute | solution.py:333
  215.9 15.7 %collective-permute-start.64 = (bf16[1,4,192,128]{3,2,1,0:T(8,128)(2,1)S(1)}, bf16[1,4,192,128]{3,2,1,0:T(8,128)(2,1)S(1)}, u32[]{:S(2)}, u32[]{:S(2)}) collective-permute-start(bf16[1,4,192,128]{3,2,1,0:T(8,128)(2,1)S(1)} %fusion.6), channel_id=1, source_target_pairs={{0,8},{4,12},{8,0},{12,4},{16,24},{20,28},{24,16},{28,20},{1,9},{5... | collective-permute-start | bytes 589832 | tf_op jit(solution)/shard_map/ppermute | solution.py:333
  220.7 11.6 %collective-permute-start.37 = (bf16[1,4,192,128]{3,2,1,0:T(8,128)(2,1)S(1)}, bf16[1,4,192,128]{3,2,1,0:T(8,128)(2,1)S(1)}, u32[]{:S(2)}, u32[]{:S(2)}) collective-permute-start(bf16[1,4,192,128]{3,2,1,0:T(8,128)(2,1)S(1)} %fusion.16), channel_id=1, source_target_pairs={{0,16},{4,20},{8,24},{12,28},{16,0},{20,4},{24,8},{28,12},{1,17},{... | collective-permute-start | bytes 589832 | tf_op jit(solution)/shard_map/ppermute | solution.py:333
  261.0 10.0 %collective-permute-start.30 = (bf16[2,96,768]{2,1,0:T(8,128)(2,1)S(1)}, bf16[2,96,768]{2,1,0:T(8,128)(2,1)S(1)}, u32[]{:S(2)}, u32[]{:S(2)}) collective-permute-start(bf16[2,96,768]{2,1,0:T(8,128)(2,1)S(1)} %get-tuple-element.96), channel_id=1, source_target_pairs={{0,8},{4,12},{8,0},{12,4},{16,24},{20,28},{24,16},{28,20},{1,9},{5... | collective-permute-start | bytes 884744 | tf_op jit(solution)/shard_map/ppermute | solution.py:333
  268.9 9.4 %collective-permute-start.21 = (bf16[2,96,768]{2,1,0:T(8,128)(2,1)S(1)}, bf16[2,96,768]{2,1,0:T(8,128)(2,1)S(1)}, u32[]{:S(2)}, u32[]{:S(2)}) collective-permute-start(bf16[2,96,768]{2,1,0:T(8,128)(2,1)S(1)} %get-tuple-element.101), channel_id=1, source_target_pairs={{0,8},{4,12},{8,0},{12,4},{16,24},{20,28},{24,16},{28,20},{1,9},{5... | collective-permute-start | bytes 884744 | tf_op jit(solution)/shard_map/ppermute | solution.py:333
  272.5 12.8 %collective-permute-start.26 = (bf16[1,96,768]{2,1,0:T(8,128)(2,1)S(1)}, bf16[1,96,768]{2,1,0:T(8,128)(2,1)S(1)}, u32[]{:S(2)}, u32[]{:S(2)}) collective-permute-start(bf16[1,96,768]{2,1,0:T(8,128)(2,1)S(1)} %fusion.24), channel_id=1, source_target_pairs={{0,8},{4,12},{8,0},{12,4},{16,24},{20,28},{24,16},{28,20},{1,9},{5... | collective-permute-start | bytes 442376 | tf_op jit(solution)/shard_map/ppermute | solution.py:333
  279.7 8.8 %collective-permute-start.32 = (bf16[96,192]{1,0:T(8,128)(2,1)S(1)}, bf16[96,192]{1,0:T(8,128)(2,1)S(1)}, u32[]{:S(2)}, u32[]{:S(2)}) collective-permute-start(bf16[96,192]{1,0:T(8,128)(2,1)S(1)} %get-tuple-element.156), channel_id=1, source_target_pairs={{0,1},{1,0},{2,3},{3,2},{4,5},{5,4},{6,7},{7,6},{8,9},{9,8},{10,11... | collective-permute-start | bytes 110600 | tf_op jit(solution)/shard_map/ppermute | solution.py:379
  280.0 10.0 %collective-permute-start.33 = (bf16[96,192]{1,0:T(8,128)(2,1)S(1)}, bf16[96,192]{1,0:T(8,128)(2,1)S(1)}, u32[]{:S(2)}, u32[]{:S(2)}) collective-permute-start(bf16[96,192]{1,0:T(8,128)(2,1)S(1)} %get-tuple-element.158), channel_id=1, source_target_pairs={{0,2},{1,3},{2,0},{3,1},{4,6},{5,7},{6,4},{7,5},{8,10},{9,11},{10,... | collective-permute-start | bytes 110600 | tf_op jit(solution)/shard_map/ppermute | solution.py:379
  (55 other events, 559.7 us)
